TPU v7x, 128 devices: a whole 4x4x4 slice. The times are simulated.
128 devices in a mesh: lat: 8 (over z_lo, x), lon: 16 (over y, z_hi, core).
Axes of the slice: x: 4, y: 4, z: 4 (z_hi: 2, z_lo: 2; z = z_hi * 2 + z_lo), core: 2. Of those that a mesh axis runs over, the one named last changes fastest.
Arguments:
- background: float32 [2, 25, 512, 2048], P(None, None, 'lat', 'lon'), may hold values from -6 to 6
- error_scale: float32 [2, 25, 512, 2048], P(None, None, 'lat', 'lon'), may hold values from 0.5 to 2
- east_rate: float32 [512, 2048], P('lat', 'lon'), may hold values from 0.05 to 0.24
- north_rate: float32 [512, 2048], P('lat', 'lon'), may hold values from 0.05 to 0.24
- sea_mask: int32 [512, 2048], P('lat', 'lon'), may hold values 0 or 1
- partner: int32 [2048], replicated, may hold values from 0 to 2047, as said below
- obs_weight: float32 [128, 128, 50, 128], P(('lat', 'lon')), may hold values from -0.875 to 0.875
- obs_value: float32 [128, 128, 128], P(('lat', 'lon')), may hold values from -8 to 8
- obs_error: float32 [128, 128, 128], P(('lat', 'lon')), may hold values from 0.5 to 2
- obs_column: int32 [128, 128, 128], P(('lat', 'lon')), may hold values from 0 to 8191
- obs_count: int32 [128, 128], P(('lat', 'lon')), may hold values from 0 to 128, as said below
Outputs:
- increment: float32 [2, 25, 512, 2048], P(None, None, 'lat', 'lon')
- cost_share: float32 [], replicated
Inputs may be any that keep to these rules, and one draw needn't show every extreme that they name: `obs_count`: every source device fills all 128 slots to at least one owner, and one owner gets all 128 slots from every source. partner[g] = (s - g) modulo 2048 for one s, so partner[partner[g]] = g.
All inputs are finite; a program needn't handle non-finite values. No bound on the sum of `sea_mask` on one device may be relied on, other than what follows from the above.
Results may differ from a plain program's by a relative error of at most 0.0003.
Values sent between devices are 32-bit elements; how exact they have to be, the bound alone decides.
No kernel may reach another device: no remote copies, remote signals or barrier semaphores. Data moves between devices by JAX's collectives and lax.ppermute only.
A program may use at most 128 MiB of HBM per device.

v0:
```python
import jax
import jax.numpy as jnp
from jax import lax
from jax.experimental import pallas as pl
from jax.experimental.pallas import tpu as pltpu
from jax.sharding import PartitionSpec as P

STEPS = 4
HALO = 4
HUBER_EDGE = 1.5
F32 = jnp.float32
BF16 = jnp.bfloat16
WIDE = 2048
DEEP = 56
UNROLL_DIFFUSE = 7
VMEM_LIMIT = 56 * 1024 * 1024


def pack(
    partner_ref,
    count_ref,
    w_ref,
    value_ref,
    error_ref,
    cell_ref,
    bg_ref,
    out_ref,
    bgm_ref,
    info_ref,
    order_ref,
    counts_ref,
):
    levels, some, n = w_ref.shape
    owners = order_ref.shape[0]
    lane8 = lax.broadcasted_iota(jnp.int32, (8, n), 1)

    @pl.when(pl.program_id(0) == 0)
    def _():
        counts = jnp.transpose(jnp.broadcast_to(count_ref[...].astype(F32), (owners, n)))
        lane = lax.broadcasted_iota(jnp.int32, (owners, n), 1)
        cell = cell_ref[...]
        row = cell >> 7
        key = (((row >> 3) & 3) << 11) | ((row >> 5) << 10) | ((row & 7) << 7) | (cell & 127)
        counts_ref[...] = counts.astype(jnp.int32)
        filled = lane.astype(F32) < counts
        spread = (lane.astype(F32) - counts + 0.5) * (8192.0 / jnp.maximum(n - counts, 1.0))
        key = jnp.where(filled, key, jnp.clip(spread, 0.0, 8191.0).astype(jnp.int32))
        x = (key * n + lane).astype(F32)
        size = 2
        while size <= n:
            step = size // 2
            while step >= 1:
                first = (lane & step) == 0
                other = jnp.where(first, pltpu.roll(x, n - step, axis=1), pltpu.roll(x, step, axis=1))
                least = first == ((lane & size) == 0)
                x = jnp.where(least, jnp.minimum(x, other), jnp.maximum(x, other))
                step //= 2
            size *= 2
        order_ref[...] = x.astype(jnp.int32) & (n - 1)

    span = n * lax.axis_size("lon")
    moved = (partner_ref[0] + (span - 3)) % span
    lat_at = lax.axis_index("lat")
    info_ref[0] = moved % n
    info_ref[1] = 1 - lat_at % 2
    info_ref[2] = (lat_at == lax.axis_size("lat") - 1).astype(jnp.int32)
    info_ref[3] = moved // n

    for p in range(2):
        for k in range(0, levels, 2):
            x = jnp.concatenate([bg_ref[k, p, 0], bg_ref[k + 1, p, 0]], axis=0)
            hi = x.astype(BF16)
            at = p * 8 * levels + 8 * k
            bgm_ref[at : at + 16, 0:128] = hi
            bgm_ref[at : at + 16, 128:256] = (x - hi.astype(F32)).astype(BF16)

    for o in range(0, some, 8):
        at = pl.ds(pl.multiple_of(pl.program_id(0) * some + o, 8), 8)
        order = order_ref[at, :]
        valid = order < counts_ref[at, :]

        def put(k, v):
            out_ref[pl.ds(o * 56 + k, 8, stride=56), :] = v

        for k in range(levels):
            put(k, jnp.take_along_axis(w_ref[k, o : o + 8, :], order, axis=1))
        put(levels, jnp.take_along_axis(value_ref[at, :], order, axis=1))
        error = jnp.take_along_axis(error_ref[at, :], order, axis=1)
        put(levels + 1, jnp.where(valid, 1.0 / error, 0.0))
        put(levels + 2, jnp.take_along_axis(cell_ref[at, :], order, axis=1).astype(F32))
        for k in range(levels + 3, 56):
            put(k, jnp.zeros((8, n), F32))


def pack_call(partner, count, weight, value, error, column, bg):
    levels, owners, n = weight.shape
    ny, nx = bg.shape[1], bg.shape[2]
    steps = 4
    some = owners // steps
    whole = lambda i: (0, 0)
    return pl.pallas_call(
        pack,
        grid=(steps,),
        out_shape=(
            jax.ShapeDtypeStruct((owners * DEEP, n), F32),
            jax.ShapeDtypeStruct((levels * ny, 2 * nx), BF16),
            jax.ShapeDtypeStruct((4,), jnp.int32),
        ),
        in_specs=[
            smem(),
            pl.BlockSpec((1, owners), whole),
            pl.BlockSpec((levels, some, n), lambda i: (0, i, 0)),
            pl.BlockSpec((owners, n), whole),
            pl.BlockSpec((owners, n), whole),
            pl.BlockSpec((owners, n), whole),
            pl.BlockSpec((levels, 2, 1, 8, nx), lambda i: (0, 0, i, 0, 0)),
        ],
        out_specs=(
            pl.BlockSpec((some * DEEP, n), lambda i: (i, 0)),
            pl.BlockSpec((levels * ny // steps, 2 * nx), lambda i: (i, 0)),
            smem(),
        ),
        scratch_shapes=[pltpu.VMEM((owners, n), jnp.int32), pltpu.VMEM((owners, n), jnp.int32)],
        compiler_params=params(),
        name="pack",
    )(partner, count, weight, value, error, column, bg.reshape(levels, 2, 4, 8, nx))


def observe(rec_ref, bgm_ref, east_ref, north_ref, sea_ref, es_ref, state_ref, to_east_ref, to_west_ref, total_ref, tiles, force, whi, wlo, amat, cost_ref):
    levels = es_ref.shape[0]
    sources = rec_ref.shape[0] // 56
    rows_in = 8 * levels
    wide = whi.shape[1]
    total = tiles.shape[2]

    force[...] = jnp.zeros_like(force)
    cost_ref[...] = jnp.zeros_like(cost_ref)

    def regroup(eight, _):
        lane = lax.broadcasted_iota(jnp.int32, (8, 128), 1)
        for r in range(0, 56, 8):
            xs = [rec_ref[pl.ds(pl.multiple_of((eight * 8 + i) * 56 + r, 8), 8), :] for i in range(8)]
            for d in (1, 2, 4):
                keep = (lane // (16 * d)) % 2 == 0
                new = list(xs)
                for i in range(8):
                    if i & d == 0:
                        lo, hi = xs[i], xs[i + d]
                        new[i] = jnp.where(keep, lo, pltpu.roll(hi, 16 * d, axis=1))
                        new[i + d] = jnp.where(keep, pltpu.roll(lo, 128 - 16 * d, axis=1), hi)
                xs = new
            for i in range(8):
                tiles[i, r : r + 8, pl.ds(pl.multiple_of(eight * 128, 128), 128)] = xs[i]
        return 0

    lax.fori_loop(0, sources // 8, regroup, 0)

    iota8 = lax.broadcasted_iota(jnp.int32, (8, wide), 0)

    def tile(t, _):
        q = t // (total // wide)
        at_r = pl.ds(pl.multiple_of((t % (total // wide)) * wide, wide), wide)
        value = tiles[q, levels : levels + 1, at_r]
        inverse = tiles[q, levels + 1 : levels + 2, at_r]
        cell = tiles[q, levels + 2 : levels + 3, at_r].astype(jnp.int32)
        row = cell >> 7
        col = cell & 127
        part = row >> 5
        block = (row >> 3) & 3
        group = 2 * block + part
        valid = inverse > 0.0
        gmin = jnp.min(jnp.where(valid, group, 8))
        gmax = jnp.max(jnp.where(valid, group, -1))
        rmask = iota8 == (row & 7)
        iota128 = lax.broadcasted_iota(jnp.int32, (128, wide), 0)
        pick = jnp.where(iota128 == col, 1.0, 0.0)
        partf = part.astype(F32)
        pickb = pick.astype(BF16)
        pick2 = jnp.concatenate([pickb, pickb], axis=0)

        def sample(g, acc):
            s = jnp.dot(
                bgm_ref[pl.ds(pl.multiple_of(g * rows_in, 16), rows_in), :],
                pick2,
                preferred_element_type=F32,
            )
            parts = [None] * 4
            for k in range(levels):
                x = tiles[q, k : k + 1, at_r] * s[8 * k : 8 * k + 8, :]
                parts[k % 4] = x if parts[k % 4] is None else parts[k % 4] + x
            total_g = (parts[0] + parts[1]) + (parts[2] + parts[3])
            return acc + jnp.where(group == g, total_g, 0.0)

        acc = lax.fori_loop(gmin, gmax + 1, sample, jnp.zeros((8, wide), F32))
        equiv = jnp.sum(jnp.where(rmask, acc, 0.0), axis=0, keepdims=True)
        scaled = (value - equiv) * inverse
        magnitude = jnp.abs(scaled)
        cost_ref[...] += jnp.where(
            magnitude <= HUBER_EDGE,
            0.5 * scaled * scaled,
            HUBER_EDGE * magnitude - 0.5 * HUBER_EDGE * HUBER_EDGE,
        )
        response = HUBER_EDGE / jnp.maximum(magnitude, HUBER_EDGE) * scaled * inverse
        wr = tiles[q, 0:levels, at_r] * response
        hi = wr.astype(BF16).astype(F32)
        whi[0:levels, :] = hi
        wlo[0:levels, :] = wr - hi
        low = pick * partf
        place = jnp.concatenate([(pick - low).astype(BF16), low.astype(BF16)], axis=0)
        place2 = jnp.concatenate([place, place], axis=1)

        def spread(b, _):
            m = jnp.where(rmask & (block == b), 1.0, 0.0)
            for k in range(0, levels, 2):
                for half, src in ((0, whi), (wide, wlo)):
                    x = jnp.concatenate([m * src[k : k + 1, :], m * src[k + 1 : k + 2, :]], axis=0)
                    amat[8 * k : 8 * k + 16, half : half + wide] = x.astype(BF16)
            at = pl.ds(pl.multiple_of(b * rows_in, 8), rows_in)
            force[at, :] += lax.dot_general(
                amat[...], place2, (((1,), (1,)), ((), ())), preferred_element_type=F32
            )
            return 0

        lax.fori_loop(gmin >> 1, (gmax >> 1) + 1, spread, 0)
        return 0

    lax.fori_loop(0, 8 * (total // wide), tile, 0)

    total_ref[...] = jnp.broadcast_to(jnp.sum(cost_ref[...], axis=1, keepdims=True)[None], total_ref.shape)

    for r0 in range(0, 64, 8):
        b, part = (r0 // 8) % 4, r0 // 32
        sea = sea_ref[r0 : r0 + 8, :].astype(F32)

        def level_rows(k):
            return pl.ds(r0 * DEEP + k, 8, stride=DEEP)

        state_ref[level_rows(levels), :] = east_ref[r0 : r0 + 8, :]
        state_ref[level_rows(levels + 1), :] = north_ref[r0 : r0 + 8, :]
        state_ref[level_rows(levels + 2), :] = sea
        for k in range(levels + 3, DEEP):
            state_ref[level_rows(k), :] = jnp.zeros((8, 128), F32)
        for k in range(levels):
            f = force[b * rows_in + 8 * k : b * rows_in + 8 * k + 8, 128 * part : 128 * part + 128]
            state_ref[level_rows(k), :] = sea * es_ref[k, r0 : r0 + 8, :] * f

    lane = lax.broadcasted_iota(jnp.int32, (8, 128), 1)

    def messages(g, _):
        def row(r):
            return state_ref[pl.ds(pl.multiple_of(r * DEEP + 8 * g, 8), 8), :]

        here = pl.ds(pl.multiple_of(8 * g, 8), 8)
        for half in range(2):
            last = jnp.zeros((8, 128), F32)
            first = jnp.zeros((8, 128), F32)
            for i in range(32):
                x = row(32 * half + i)
                mine = (lane >> 2) == i
                last = jnp.where(mine, pltpu.roll(x, (4 * i + 4) % 128, axis=1), last)
                first = jnp.where(mine, pltpu.roll(x, 4 * i, axis=1), first)
            to_east_ref[here, 128 * half : 128 * half + 128] = last
            to_west_ref[here, 128 * half : 128 * half + 128] = first
        more = jnp.zeros((8, 128), F32)
        for d in range(4):
            x = row(60 + d)
            to_east_ref[here, 256 + 128 * d : 384 + 128 * d] = x
            more = jnp.where((lane >> 2) == d, pltpu.roll(x, (4 * d - 4) % 128, axis=1), more)
        to_west_ref[here, 256:384] = more
        return 0

    lax.fori_loop(0, DEEP // 8, messages, 0)


def observe_call(received, bgm, east_rate, north_rate, sea_mask, es, wide=WIDE):
    levels, ny, nx = es.shape
    owners = received.shape[0] // 56
    return pl.pallas_call(
        observe,
        out_shape=(
            jax.ShapeDtypeStruct((ny * DEEP, nx), F32),
            jax.ShapeDtypeStruct((DEEP, 768), F32),
            jax.ShapeDtypeStruct((DEEP, 384), F32),
            jax.ShapeDtypeStruct((owners, 1, 128), F32),
        ),
        in_specs=[vmem()] * 6,
        out_specs=(vmem(),) * 4,
        scratch_shapes=[
            pltpu.VMEM((8, 56, 16 * owners), F32),
            pltpu.VMEM((32 * levels, 256), F32),
            pltpu.VMEM((56, wide), F32),
            pltpu.VMEM((56, wide), F32),
            pltpu.VMEM((8 * levels, 2 * wide), BF16),
            pltpu.VMEM((1, wide), F32),
        ],
        compiler_params=params(),
        name="observe",
    )(received, bgm, east_rate, north_rate, sea_mask, es)


def side_tile(fe, fw, r, lane):
    half, i = r // 32, r % 32
    e = pltpu.roll(fe[128 * half], (128 - 4 * i) % 128, axis=1)
    w = pltpu.roll(fw[128 * half], (124 - 4 * i) % 128, axis=1)
    return jnp.where(lane < 64, e, w)


def assemble(info_ref, bot_ref, top_ref, fw_ref, fe_ref, one_ref, two_ref):
    shift = info_ref[0]
    even = info_ref[1] == 1
    fold = info_ref[2] == 1
    lane = lax.broadcasted_iota(jnp.int32, (8, 128), 1)
    rel_a = shift + 3 - lane
    rel_b = jnp.where(lane < 64, shift + 3 - 128 - lane, shift + 3 + 128 - lane)

    def mirror(west, own, east, rel):
        idx = rel & 127
        w = jnp.take_along_axis(west, idx, axis=1)
        o = jnp.take_along_axis(own, idx, axis=1)
        e = jnp.take_along_axis(east, idx, axis=1)
        return jnp.where(rel < 0, w, jnp.where(rel < 128, o, e))

    def body(g, _):
        here = pl.ds(pl.multiple_of(8 * g, 8), 8)
        fe = {c: fe_ref[here, c : c + 128] for c in (0, 128, 256)}
        fw = {c: fw_ref[here, c : c + 128] for c in range(0, 768, 128)}
        top = [top_ref[d, here, :] for d in range(4)]
        top_side = [side_tile(fe, fw, 60 + d, lane) for d in range(4)]
        sides = [jnp.zeros((8, 128), F32) for _ in range(3)]
        for d in range(4):
            u = 3 - d
            east = jnp.where(lane < 4, top_side[u], pltpu.roll(fe[256], (4 - 4 * u) % 128, axis=1))
            fold_a = mirror(fw[256 + 128 * u], top[u], east, rel_a)
            fold_b = mirror(fw[256 + 128 * u], top[u], east, rel_b)
            bot = bot_ref[d, here, :]
            one_ref[d, here, :] = jnp.where(even, top[d], bot)
            two_ref[d, here, :] = jnp.where(even, bot, jnp.where(fold, fold_a, top[d]))
            for n, x in enumerate((top_side[d], side_tile(fe, fw, d, lane), fold_b)):
                sides[n] = jnp.where((lane >> 3) == d, pltpu.roll(x, 8 * d + 4, axis=1), sides[n])
        one_ref[4, here, :] = jnp.where(even, sides[0], sides[1])
        two_ref[4, here, :] = jnp.where(even, sides[1], jnp.where(fold, sides[2], sides[0]))
        return 0

    lax.fori_loop(0, DEEP // 8, body, 0)


def diffuse(info_ref, x_ref, fw_ref, fe_ref, one_ref, two_ref, es_ref, out_ref, sa, sb, coef):
    levels = es_ref.shape[0] // 64
    even = info_ref[1] == 1
    lane = lax.broadcasted_iota(jnp.int32, (8, 128), 1)

    def fill(g, _):
        here = pl.ds(pl.multiple_of(8 * g, 8), 8)
        fe = {c: fe_ref[here, c : c + 128] for c in (0, 128)}
        fw = {c: fw_ref[here, c : c + 128] for c in (0, 128)}
        for r in range(64):
            sa[r + 4, here, 0:128] = x_ref[r, here, :]
            sa[r + 4, here, 128:256] = side_tile(fe, fw, r, lane)
        for d in range(4):
            one = one_ref[d, here, :]
            two = two_ref[d, here, :]
            sa[d, here, 0:128] = jnp.where(even, two, one)
            sa[68 + d, here, 0:128] = jnp.where(even, one, two)
            one = pltpu.roll(one_ref[4, here, :], 124 - 8 * d, axis=1)
            two = pltpu.roll(two_ref[4, here, :], 124 - 8 * d, axis=1)
            sa[d, here, 128:256] = jnp.where(even, two, one)
            sa[68 + d, here, 128:256] = jnp.where(even, one, two)
        return 0

    lax.fori_loop(0, DEEP // 8, fill, 0)

    rows, cols = sa.shape[0], sa.shape[2]
    col = lax.broadcasted_iota(jnp.int32, (rows, cols), 1)
    live = (col < 132) | (col >= 252)
    sea = jnp.where(live, sa[:, levels + 2, :], 0.0)
    east = jnp.where(live, sa[:, levels, :], 0.0) * sea
    north = jnp.where(live, sa[:, levels + 1, :], 0.0) * sea
    a_e = east * pltpu.roll(sea, cols - 1, axis=1)
    a_w = east * pltpu.roll(sea, 1, axis=1)
    a_n = north * pltpu.roll(sea, rows - 1, axis=0)
    a_s = north * pltpu.roll(sea, 1, axis=0)
    coef[0] = 1.0 - ((a_e + a_w) + (a_n + a_s))
    coef[1] = a_e
    coef[2] = a_w
    coef[3] = a_n
    coef[4] = a_s

    def step(src, lo, hi, put):
        def body(r, _):
            c = [coef[i, pl.ds(r, 1), :] for i in range(5)]
            for g in range(DEEP // 8):
                here = slice(8 * g, 8 * g + 8)
                s = src[r, here, :]
                put(
                    r,
                    g,
                    c[0] * s
                    + (c[1] * pltpu.roll(s, cols - 1, axis=1) + c[2] * pltpu.roll(s, 1, axis=1))
                    + (c[3] * src[r + 1, here, :] + c[4] * src[r - 1, here, :]),
                )
            return 0

        lax.fori_loop(lo, hi, body, 0, unroll=UNROLL_DIFFUSE)

    def keep(dst):
        def put(r, g, v):
            dst[r, 8 * g : 8 * g + 8, :] = v

        return put

    def finish(r, g, v):
        n = min(8, levels - 8 * g)
        at = pl.ds(8 * g * 64 + r - 4, n, stride=64)
        out_ref[at, :] = es_ref[at, :] * v[0:n, 0:128]

    step(sa, 1, 71, keep(sb))
    step(sb, 2, 70, keep(sa))
    step(sa, 3, 69, keep(sb))
    step(sb, 4, 68, finish)


def vmem():
    return pl.BlockSpec(memory_space=pltpu.VMEM)


def smem():
    return pl.BlockSpec(memory_space=pltpu.SMEM)


def params():
    return pltpu.CompilerParams(vmem_limit_bytes=VMEM_LIMIT)


def perm_of(n_lat, n_lon, rule):
    pairs = []
    for a in range(n_lat):
        for b in range(n_lon):
            to = rule(a, b)
            if to is not None:
                pairs.append((a * n_lon + b, to[0] * n_lon + to[1] % n_lon))
    return pairs


def assemble_call(info, state, from_west, from_east):
    rows = jax.ShapeDtypeStruct((5, DEEP, 128), F32)
    return pl.pallas_call(
        assemble,
        grid=(1,),
        out_shape=(rows, rows),
        in_specs=[
            smem(),
            pl.BlockSpec((4, DEEP, 128), lambda i: (0, 0, 0)),
            pl.BlockSpec((4, DEEP, 128), lambda i: (15, 0, 0)),
            vmem(),
            vmem(),
        ],
        out_specs=(vmem(), vmem()),
        compiler_params=params(),
        name="assemble",
    )(info, state, state, from_west, from_east)


def diffuse_call(info, state, from_west, from_east, one, two, es):
    levels, ny, nx = es.shape
    out = pl.pallas_call(
        diffuse,
        out_shape=jax.ShapeDtypeStruct((levels * ny, nx), F32),
        in_specs=[smem()] + [vmem()] * 6,
        out_specs=vmem(),
        scratch_shapes=[
            pltpu.VMEM((ny + 8, DEEP, 2 * nx), F32),
            pltpu.VMEM((ny + 8, DEEP, 2 * nx), F32),
            pltpu.VMEM((5, ny + 8, 2 * nx), F32),
        ],
        compiler_params=params(),
        cost_estimate=pl.CostEstimate(flops=20 * STEPS * levels * ny * nx, bytes_accessed=60000000, transcendentals=0),
        name="diffuse",
    )(info, state, from_west, from_east, one, two, es.reshape(levels * ny, nx))
    return out.reshape(levels, ny, nx)


def shards(
    background,
    error_scale,
    east_rate,
    north_rate,
    sea_mask,
    partner,
    obs_weight,
    obs_value,
    obs_error,
    obs_column,
    obs_count,
):
    levels = background.shape[0] * background.shape[1]
    ny = background.shape[2]
    nx = background.shape[3]
    capacity = obs_weight.shape[3]
    owners = obs_weight.shape[1]
    bg = background.reshape(levels, ny, nx)
    es = error_scale.reshape(levels, ny, nx)
    packed, bgm, info = pack_call(
        partner, obs_count, jnp.swapaxes(obs_weight[0], 0, 1), obs_value[0], obs_error[0], obs_column[0], bg
    )
    turn = info[3]
    packed, bgm, info, turn = lax.optimization_barrier((packed, bgm, info, turn))
    received = lax.all_to_all(packed, ("lat", "lon"), split_axis=0, concat_axis=0, tiled=True)
    state, to_east, to_west, cost = observe_call(received, bgm, east_rate, north_rate, sea_mask, es)
    state = state.reshape(ny, DEEP, nx)

    n_lat = lax.axis_size("lat")
    n_lon = lax.axis_size("lon")
    from_west = lax.ppermute(to_east, "lon", [(i, (i + 1) % n_lon) for i in range(n_lon)])
    from_east = lax.ppermute(to_west, "lon", [((i + 1) % n_lon, i) for i in range(n_lon)])
    one, two = assemble_call(info, state, from_west, from_east)

    def branch(q):
        def rule(a, b):
            if a == n_lat - 1:
                return (a, q - b)
            if a == 0:
                return None
            return (((a + 1) ^ 1) - 1, b)

        def run(one, two, cost):
            got_one = lax.ppermute(one, ("lat", "lon"), perm_of(n_lat, n_lon, lambda a, b: (a ^ 1, b)))
            got_two = lax.ppermute(two, ("lat", "lon"), perm_of(n_lat, n_lon, rule))
            shares = lax.all_to_all(cost, ("lat", "lon"), split_axis=0, concat_axis=0, tiled=True)
            return got_one, got_two, shares

        return run

    got_one, got_two, shares = lax.switch(turn, [branch(q) for q in range(n_lon)], one, two, cost)
    cost_share = jnp.sum(shares[:, 0, 0]) / (owners * owners * capacity)
    increment = diffuse_call(info, state, from_west, from_east, got_one, got_two, es)
    return (increment.reshape(background.shape), cost_share)


def solution(mesh):
    in_specs = (
        P(None, None, "lat", "lon"),
        P(None, None, "lat", "lon"),
        P("lat", "lon"),
        P("lat", "lon"),
        P("lat", "lon"),
        P(),
        P(("lat", "lon"), None, None, None),
        P(("lat", "lon"), None, None),
        P(("lat", "lon"), None, None),
        P(("lat", "lon"), None, None),
        P(("lat", "lon"), None),
    )
    out_specs = (P(None, None, "lat", "lon"), P())
    return jax.shard_map(shards, mesh=mesh, in_specs=in_specs, out_specs=out_specs, check_vma=False)
```

profile of v0, /device:TPU:6, one launch (start us, length us, event | category | flops | bytes accessed | tf_op | source)
XLA Modules:
  0.0 164.1 jit_solution(6578248393987849454)
XLA Ops:
  0.6 7.8 %pack.1 = (f32[7168,128]{1,0:T(8,128)}, bf16[3200,256]{1,0:T(8,128)(2,1)}, s32[4]{0:T(128)}) custom-call(s32[2048]{0:T(1024)} %partner_ref.1, s32[1,128]{1,0:T(1,128)} %count_ref.1, f32[50,128,128]{2,1,0:T(8,128)} %bitcast.21, f32[128,128]{1,0:T(8,128)} %bitcast.24, f32[128,128]{1,0:T(8,128)} %bitcast.25, s32[128,128]{1,0:T(8,128)} %bitcast.26, ...), custom_call_target="tpu_custom_call" | custom-call | tf_op jit(solution)/shard_map/pack/pallas_call | solution.py:101
  8.5 1.2 slice.52
  9.7 56.2 %all_to_all.75 = f32[128,56,128]{2,1,0:T(8,128)} all-to-all(f32[128,56,128]{2,1,0:T(8,128)} %bitcast.20), channel_id=1, replica_groups=mesh['lat'=8,'lon'=16] {'lat','lon'}, dimensions={0} | all-to-all | bytes 7340032 | tf_op jit(solution)/shard_map/all_to_all | solution.py:507
  65.9 48.1 %observe.1 = (f32[3584,128]{1,0:T(8,128)}, f32[56,768]{1,0:T(8,128)}, f32[56,384]{1,0:T(8,128)}, f32[128,1,128]{2,1,0:T(1,128)}) custom-call(f32[7168,128]{1,0:T(8,128)} %bitcast.17, bf16[3200,256]{1,0:T(8,128)(2,1)} %get-tuple-element.168.bgm_ref, f32[64,128]{1,0:T(8,128)} %east_ref.1, f32[64,128]{1,0:T(8,128)} %north_ref.1, s32[64,128]{1,0:T(8,128)} %sea_ref.1, ...), custom_call_target="tpu_custom_call" | custom-call | tf_op jit(solution)/shard_map/observe/pallas_call | solution.py:278
  114.0 0.0 collective-permute-start.32
  114.0 5.4 %collective-permute-start.33 = (f32[56,384]{1,0:T(8,128)}, f32[56,384]{1,0:T(8,128)S(1)}, u32[]{:S(2)}, u32[]{:S(2)}) collective-permute-start(f32[56,384]{1,0:T(8,128)} %get-tuple-element.171), channel_id=1, source_target_pairs={{1,0},{2,1},{3,2},{4,3},{5,4},{6,5},{7,6},{8,7},{9,8},{10,9},{11,1... | collective-permute-start | bytes 258056 | tf_op jit(solution)/shard_map/ppermute | solution.py:514
  120.1 1.8 %collective-permute-done.33.fe_ref = f32[56,384]{1,0:T(8,128)S(1)} collective-permute-done((f32[56,384]{1,0:T(8,128)}, f32[56,384]{1,0:T(8,128)S(1)}, u32[]{:S(2)}, u32[]{:S(2)}) %collective-permute-start.33) | collective-permute-done | bytes 86048 | tf_op jit(solution)/shard_map/ppermute | solution.py:514
  121.8 0.0 copy-start.1
  121.8 0.9 collective-permute-done.32.fw_ref
  122.7 0.0 copy-start
  122.7 0.0 copy-done.1
  122.7 0.7 copy-done
  123.4 2.7 %assemble.1 = (f32[5,56,128]{2,1,0:T(8,128)S(1)}, f32[5,56,128]{2,1,0:T(8,128)S(1)}) custom-call(s32[4]{0:T(128)} %get-tuple-element.166.info_ref, f32[64,56,128]{2,1,0:T(8,128)} %bitcast.14, f32[64,56,128]{2,1,0:T(8,128)} %bitcast.15, f32[56,768]{1,0:T(8,128)} %copy-done, f32[56,384]{1,0:T(8,128)} %copy-done.1), custom_call_target="tpu_custom_call" | custom-call | tf_op jit(solution)/shard_map/assemble/pallas_call | solution.py:446
  126.0 19.5 %conditional.1 = (f32[5,56,128]{2,1,0:T(8,128)}, f32[5,56,128]{2,1,0:T(8,128)}, f32[]{:T(128)}) conditional(s32[]{:T(128)} %clamp.3, (f32[5,56,128]{2,1,0:T(8,128)S(1)}, f32[5,56,128]{2,1,0:T(8,128)S(1)}, f32[128,1,128]{2,1,0:T(1,128)}) %tuple.90, (f32[5,56,128]{2,1,0:T(8,128)S(1)}, f32[5,56,128]{2,1,0:T(8,128)S(1)}, ...), branch_computations={%region_0.2_spmd, %region_2.4_spmd, %region_4.6_spmd, %region_6.8_... | conditional | flops 128 | bytes 1344152 | solution.py:533
  126.0 8.0 %all-to-all-start = ((f32[128,1,128]{2,1,0:T(1,128)}), f32[128,1,128]{2,1,0:T(1,128)S(1)}, u32[]{:S(2)}, u32[]{:S(2)}) async-start(f32[128,1,128]{2,1,0:T(1,128)} %get-tuple-element.99), calls=%async_computation | async-start | bytes 131072 | tf_op jit(solution)/shard_map/cond/branch_0_fun/all_to_all | solution.py:528
  134.1 0.9 collective-permute-start
  135.0 4.1 %collective-permute-start.1 = (f32[5,56,128]{2,1,0:T(8,128)S(1)}, f32[5,56,128]{2,1,0:T(8,128)}, u32[]{:S(2)}, u32[]{:S(2)}) collective-permute-start(f32[5,56,128]{2,1,0:T(8,128)S(1)} %get-tuple-element.98), channel_id=1, source_target_pairs={{16,32},{17,33},{18,34},{19,35},{20,36},{21,37},{22,38},{23,39},{2... | collective-permute-start | bytes 430088 | tf_op jit(solution)/shard_map/cond/branch_0_fun/ppermute | solution.py:527
  139.1 2.9 %all-to-all-done = f32[128,1,128]{2,1,0:T(1,128)S(1)} async-done(((f32[128,1,128]{2,1,0:T(1,128)}), f32[128,1,128]{2,1,0:T(1,128)S(1)}, u32[]{:S(2)}, u32[]{:S(2)}) %all-to-all-start) | async-done | bytes 65568 | tf_op jit(solution)/shard_map/cond/branch_0_fun/all_to_all | solution.py:528
  142.0 0.7 slice_reduce_fusion
  143.4 0.0 collective-permute-done
  143.4 2.1 %collective-permute-done.1 = f32[5,56,128]{2,1,0:T(8,128)} collective-permute-done((f32[5,56,128]{2,1,0:T(8,128)S(1)}, f32[5,56,128]{2,1,0:T(8,128)}, u32[]{:S(2)}, u32[]{:S(2)}) %collective-permute-start.1) | collective-permute-done | bytes 143392 | tf_op jit(solution)/shard_map/cond/branch_0_fun/ppermute | solution.py:527
  145.5 17.4 %diffuse.1 = f32[3200,128]{1,0:T(8,128)} custom-call(s32[4]{0:T(128)} %get-tuple-element.166.info_ref, f32[64,56,128]{2,1,0:T(8,128)} %bitcast.16, f32[56,768]{1,0:T(8,128)} %copy-done, f32[56,384]{1,0:T(8,128)} %copy-done.1, f32[5,56,128]{2,1,0:T(8,128)} %get-tuple-element.176.one_ref, f32[5,56,128]{2,1,0:T(8,128)} %get-tuple-element.177.two_ref, ...), custom_call_target="tpu_custom_call" | custom-call | flops 32768000 | bytes 60000000 | tf_op jit(solution)/shard_map/diffuse/pallas_call | solution.py:465
Async XLA Ops:
  114.0 8.7 %collective-permute-start.32 = (f32[56,768]{1,0:T(8,128)}, f32[56,768]{1,0:T(8,128)S(1)}, u32[]{:S(2)}, u32[]{:S(2)}) collective-permute-start(f32[56,768]{1,0:T(8,128)} %get-tuple-element.170), channel_id=1, source_target_pairs={{0,1},{1,2},{2,3},{3,4},{4,5},{5,6},{6,7},{7,8},{8,9},{9,10},{10,1... | collective-permute-start | bytes 516104 | tf_op jit(solution)/shard_map/ppermute | solution.py:513
  114.0 7.8 %collective-permute-start.33 = (f32[56,384]{1,0:T(8,128)}, f32[56,384]{1,0:T(8,128)S(1)}, u32[]{:S(2)}, u32[]{:S(2)}) collective-permute-start(f32[56,384]{1,0:T(8,128)} %get-tuple-element.171), channel_id=1, source_target_pairs={{1,0},{2,1},{3,2},{4,3},{5,4},{6,5},{7,6},{8,7},{9,8},{10,9},{11,1... | collective-permute-start | bytes 258056 | tf_op jit(solution)/shard_map/ppermute | solution.py:514
  121.8 0.9 copy-start.1
  122.7 0.7 copy-start
  126.0 16.0 %all-to-all-start = ((f32[128,1,128]{2,1,0:T(1,128)}), f32[128,1,128]{2,1,0:T(1,128)S(1)}, u32[]{:S(2)}, u32[]{:S(2)}) async-start(f32[128,1,128]{2,1,0:T(1,128)} %get-tuple-element.99), calls=%async_computation | async-start | bytes 131072 | tf_op jit(solution)/shard_map/cond/branch_0_fun/all_to_all | solution.py:528
  134.1 9.3 %collective-permute-start = (f32[5,56,128]{2,1,0:T(8,128)S(1)}, f32[5,56,128]{2,1,0:T(8,128)}, u32[]{:S(2)}, u32[]{:S(2)}) collective-permute-start(f32[5,56,128]{2,1,0:T(8,128)S(1)} %get-tuple-element.97), channel_id=1, source_target_pairs={{0,16},{1,17},{2,18},{3,19},{4,20},{5,21},{6,22},{7,23},{8,24},{9,... | collective-permute-start | bytes 430088 | tf_op jit(solution)/shard_map/cond/branch_0_fun/ppermute | solution.py:526
  135.0 10.5 %collective-permute-start.1 = (f32[5,56,128]{2,1,0:T(8,128)S(1)}, f32[5,56,128]{2,1,0:T(8,128)}, u32[]{:S(2)}, u32[]{:S(2)}) collective-permute-start(f32[5,56,128]{2,1,0:T(8,128)S(1)} %get-tuple-element.98), channel_id=1, source_target_pairs={{16,32},{17,33},{18,34},{19,35},{20,36},{21,37},{22,38},{23,39},{2... | collective-permute-start | bytes 430088 | tf_op jit(solution)/shard_map/cond/branch_0_fun/ppermute | solution.py:527
where the time goes:
time: 166 us; the launch traced here: 164 us
  Pallas kernels  76.1 us (46%)
  blocking collectives  56.2 us (34%)
  starting transfers between devices  18.4 us (11%)
  waiting for transfers between devices  7.64 us (5%)
  between operations  2.42 us (1%)
  local copies, waits for them, and re-layouts  1.88 us (1%)
    all_to_all x1, blocking collectives, shards(): lax.all_to_all(packed, ('lat', 'lon'), split_axis=0, concat_axis=0, tiled...  56.2 us
    pallas_call x1, Pallas kernels, observe_call(): pl.pallas_call(observe, out_shape=(jax.ShapeDtypeStruct((ny * DEEP, nx),...  48.1 us
    pallas_call x1, Pallas kernels, diffuse_call(): pl.pallas_call(diffuse, out_shape=jax.ShapeDtypeStruct((levels * ny, nx),...  17.4 us
    all_to_all x1, starting transfers between devices, run(): lax.all_to_all(cost, ('lat', 'lon'), split_axis=0, concat_axis=0, tiled=T...  8.01 us
    pallas_call x1, Pallas kernels, pack_call(): pl.pallas_call(pack, grid=(steps,), out_shape=(jax.ShapeDtypeStruct((owne...  7.84 us
    ppermute x1, starting transfers between devices, shards(): lax.ppermute(to_west, 'lon', [((i + 1) % n_lon, i) for i in range(n_lon)])  5.36 us
    ppermute x1, starting transfers between devices, run(): got_two = lax.ppermute(two, ('lat', 'lon'), perm_of(n_lat, n_lon, rule))  4.1 us
  transfers between devices with their start and end apart: 5, of which 4 were waited for; matrix products, arithmetic and copies ran while one was open for 0% of the time, Pallas kernels for 0%

commit v1 on v0

--- a/solution.py
+++ b/solution.py
@@ -514,6 +514,8 @@
     from_east = lax.ppermute(to_west, "lon", [((i + 1) % n_lon, i) for i in range(n_lon)])
     one, two = assemble_call(info, state, from_west, from_east)
 
+    shares = lax.all_to_all(cost, ("lat", "lon"), split_axis=0, concat_axis=0, tiled=True)
+
     def branch(q):
         def rule(a, b):
             if a == n_lat - 1:
@@ -522,15 +524,15 @@
                 return None
             return (((a + 1) ^ 1) - 1, b)
 
-        def run(one, two, cost):
+        def run(one, two):
             got_one = lax.ppermute(one, ("lat", "lon"), perm_of(n_lat, n_lon, lambda a, b: (a ^ 1, b)))
             got_two = lax.ppermute(two, ("lat", "lon"), perm_of(n_lat, n_lon, rule))
-            shares = lax.all_to_all(cost, ("lat", "lon"), split_axis=0, concat_axis=0, tiled=True)
-            return got_one, got_two, shares
+            return got_one, got_two
 
         return run
 
-    got_one, got_two, shares = lax.switch(turn, [branch(q) for q in range(n_lon)], one, two, cost)
+    one, two, shares = lax.optimization_barrier((one, two, shares))
+    got_one, got_two = lax.switch(turn, [branch(q) for q in range(n_lon)], one, two)
     cost_share = jnp.sum(shares[:, 0, 0]) / (owners * owners * capacity)
     increment = diffuse_call(info, state, from_west, from_east, got_one, got_two, es)
     return (increment.reshape(background.shape), cost_share)

time: 166 us -> 164 us (0.988); the launches traced: 164 us -> 164 us
  Pallas kernels: 76.1 us -> 73.8 us
  waiting for transfers between devices: 7.64 us -> 9.33 us
    ppermute x1, waiting for transfers between devices: 2.1 us -> 4.59 us  [run(): got_two = lax.ppermute(two, ('lat', 'lon'), perm_of(n_lat, n_lon, rule))]
    pallas_call x1, Pallas kernels: 48.1 us -> 45.8 us  [observe_call(): pl.pallas_call(observe, out_shape=(jax.ShapeDtypeStruct((ny * DEEP, nx),...]
    ppermute x1, waiting for transfers between devices: 1.76 us -> 0.01 us  [shards(): lax.ppermute(to_west, 'lon', [((i + 1) % n_lon, i) for i in range(n_lon)])]
  transfers between devices with their start and end apart: 5 -> 5, of which waited for: 4 -> 3; matrix products, arithmetic and copies ran while one was open for 0% -> 0% of each run, Pallas kernels for 0% -> 2%
where the time goes in v1:
time: 164 us
  Pallas kernels  73.8 us (45%)
  blocking collectives  56.2 us (34%)
  starting transfers between devices  19.3 us (12%)
  waiting for transfers between devices  9.33 us (6%)
  between operations  3.11 us (2%)
  local copies, waits for them, and re-layouts  1.82 us (1%)
    all_to_all x1, blocking collectives, shards(): lax.all_to_all(packed, ('lat', 'lon'), split_axis=0, concat_axis=0, tiled...  56.2 us
    pallas_call x1, Pallas kernels, observe_call(): pl.pallas_call(observe, out_shape=(jax.ShapeDtypeStruct((ny * DEEP, nx),...  45.8 us
    pallas_call x1, Pallas kernels, diffuse_call(): pl.pallas_call(diffuse, out_shape=jax.ShapeDtypeStruct((levels * ny, nx),...  17.4 us
    all_to_all x1, starting transfers between devices, shards(): lax.all_to_all(cost, ('lat', 'lon'), split_axis=0, concat_axis=0, tiled=T...  8.74 us
    pallas_call x1, Pallas kernels, pack_call(): pl.pallas_call(pack, grid=(steps,), out_shape=(jax.ShapeDtypeStruct((owne...  7.84 us
    ppermute x1, starting transfers between devices, shards(): lax.ppermute(to_west, 'lon', [((i + 1) % n_lon, i) for i in range(n_lon)])  5.63 us
    ppermute x1, waiting for transfers between devices, run(): got_two = lax.ppermute(two, ('lat', 'lon'), perm_of(n_lat, n_lon, rule))  4.59 us
    ppermute x1, starting transfers between devices, run(): got_two = lax.ppermute(two, ('lat', 'lon'), perm_of(n_lat, n_lon, rule))  3.97 us
  transfers between devices with their start and end apart: 5, of which 3 were waited for; matrix products, arithmetic and copies ran while one was open for 0% of the time, Pallas kernels for 2%

profile of v1, /device:TPU:6, one launch (start us, length us, event | category | flops | bytes accessed | tf_op | source)
XLA Modules:
  0.0 164.4 jit_solution(7852424117332342072)
XLA Ops:
  0.6 7.8 %pack.1 = (f32[7168,128]{1,0:T(8,128)}, bf16[3200,256]{1,0:T(8,128)(2,1)}, s32[4]{0:T(128)}) custom-call(s32[2048]{0:T(1024)} %partner_ref.1, s32[1,128]{1,0:T(1,128)} %count_ref.1, f32[50,128,128]{2,1,0:T(8,128)} %bitcast.21, f32[128,128]{1,0:T(8,128)} %bitcast.24, f32[128,128]{1,0:T(8,128)} %bitcast.25, s32[128,128]{1,0:T(8,128)} %bitcast.26, ...), custom_call_target="tpu_custom_call" | custom-call | tf_op jit(solution)/shard_map/pack/pallas_call | solution.py:101
  8.5 1.2 slice.6
  9.6 56.2 %all_to_all.16 = f32[128,56,128]{2,1,0:T(8,128)} all-to-all(f32[128,56,128]{2,1,0:T(8,128)} %bitcast.20), channel_id=1, replica_groups=mesh['lat'=8,'lon'=16] {'lat','lon'}, dimensions={0} | all-to-all | bytes 7340032 | tf_op jit(solution)/shard_map/all_to_all | solution.py:507
  65.9 45.8 %observe.1 = (f32[3584,128]{1,0:T(8,128)}, f32[56,768]{1,0:T(8,128)}, f32[56,384]{1,0:T(8,128)}, f32[128,1,128]{2,1,0:T(1,128)}) custom-call(f32[7168,128]{1,0:T(8,128)} %bitcast.17, bf16[3200,256]{1,0:T(8,128)(2,1)} %get-tuple-element.121.bgm_ref, f32[64,128]{1,0:T(8,128)} %east_ref.1, f32[64,128]{1,0:T(8,128)} %north_ref.1, s32[64,128]{1,0:T(8,128)} %sea_ref.1, ...), custom_call_target="tpu_custom_call" | custom-call | tf_op jit(solution)/shard_map/observe/pallas_call | solution.py:278
  111.7 0.0 collective-permute-start.32
  111.7 5.6 %collective-permute-start.33 = (f32[56,384]{1,0:T(8,128)}, f32[56,384]{1,0:T(8,128)S(1)}, u32[]{:S(2)}, u32[]{:S(2)}) collective-permute-start(f32[56,384]{1,0:T(8,128)} %get-tuple-element.124), channel_id=1, source_target_pairs={{1,0},{2,1},{3,2},{4,3},{5,4},{6,5},{7,6},{8,7},{9,8},{10,9},{11,1... | collective-permute-start | bytes 258056 | tf_op jit(solution)/shard_map/ppermute | solution.py:514
  117.3 8.7 %all-to-all-start.1 = ((f32[128,1,128]{2,1,0:T(1,128)}), f32[128,1,128]{2,1,0:T(1,128)S(1)}, u32[]{:S(2)}, u32[]{:S(2)}) async-start(f32[128,1,128]{2,1,0:T(1,128)} %get-tuple-element.128), calls=%async_computation.1 | async-start | bytes 131072 | tf_op jit(solution)/shard_map/all_to_all | solution.py:517
  126.7 0.0 collective-permute-done.33.fe_ref
  126.7 0.0 copy-start.1
  126.7 0.0 collective-permute-done.32.fw_ref
  126.8 0.0 copy-start
  126.8 0.6 copy-done.1
  127.4 0.1 copy-done
  127.4 2.7 %assemble.1 = (f32[5,56,128]{2,1,0:T(8,128)S(1)}, f32[5,56,128]{2,1,0:T(8,128)S(1)}) custom-call(s32[4]{0:T(128)} %get-tuple-element.119.info_ref, f32[64,56,128]{2,1,0:T(8,128)} %bitcast.14, f32[64,56,128]{2,1,0:T(8,128)} %bitcast.15, f32[56,768]{1,0:T(8,128)} %copy-done, f32[56,384]{1,0:T(8,128)} %copy-done.1), custom_call_target="tpu_custom_call" | custom-call | tf_op jit(solution)/shard_map/assemble/pallas_call | solution.py:446
  130.1 3.9 %all-to-all-done.1 = f32[128,1,128]{2,1,0:T(1,128)S(1)} async-done(((f32[128,1,128]{2,1,0:T(1,128)}), f32[128,1,128]{2,1,0:T(1,128)S(1)}, u32[]{:S(2)}, u32[]{:S(2)}) %all-to-all-start.1) | async-done | bytes 65568 | tf_op jit(solution)/shard_map/all_to_all | solution.py:517
  134.0 0.7 slice_reduce_fusion
  135.4 10.4 %conditional.1 = (f32[5,56,128]{2,1,0:T(8,128)}, f32[5,56,128]{2,1,0:T(8,128)}) conditional(s32[]{:T(128)} %clamp.3, (f32[5,56,128]{2,1,0:T(8,128)S(1)}, f32[5,56,128]{2,1,0:T(8,128)S(1)}) %assemble.1, (f32[5,56,128]{2,1,0:T(8,128)S(1)}, f32[5,56,128]{2,1,0:T(8,128)S(1)}) %assemble.1, (f32[5,56,128]{2,1,0:T(8,128)S(1)}, ...), branch_computations={%region_0.0_spmd, %region_1.0_spmd, %region_2.0_spmd, %region_3.0_... | conditional | bytes 1146976 | solution.py:535
  135.4 1.0 collective-permute-start.18
  136.4 4.0 %collective-permute-start.19 = (f32[5,56,128]{2,1,0:T(8,128)S(1)}, f32[5,56,128]{2,1,0:T(8,128)}, u32[]{:S(2)}, u32[]{:S(2)}) collective-permute-start(f32[5,56,128]{2,1,0:T(8,128)S(1)} %get-tuple-element.83), channel_id=1, source_target_pairs={{16,32},{17,33},{18,34},{19,35},{20,36},{21,37},{22,38},{23,39},{2... | collective-permute-start | bytes 430088 | tf_op jit(solution)/shard_map/cond/branch_9_fun/ppermute | solution.py:529
  140.4 0.8 collective-permute-done.18
  141.2 4.6 %collective-permute-done.19 = f32[5,56,128]{2,1,0:T(8,128)} collective-permute-done((f32[5,56,128]{2,1,0:T(8,128)S(1)}, f32[5,56,128]{2,1,0:T(8,128)}, u32[]{:S(2)}, u32[]{:S(2)}) %collective-permute-start.19) | collective-permute-done | bytes 143392 | tf_op jit(solution)/shard_map/cond/branch_9_fun/ppermute | solution.py:529
  145.8 17.4 %diffuse.1 = f32[3200,128]{1,0:T(8,128)} custom-call(s32[4]{0:T(128)} %get-tuple-element.119.info_ref, f32[64,56,128]{2,1,0:T(8,128)} %bitcast.16, f32[56,768]{1,0:T(8,128)} %copy-done, f32[56,384]{1,0:T(8,128)} %copy-done.1, f32[5,56,128]{2,1,0:T(8,128)} %get-tuple-element.131.one_ref, f32[5,56,128]{2,1,0:T(8,128)} %get-tuple-element.132.two_ref, ...), custom_call_target="tpu_custom_call" | custom-call | flops 32768000 | bytes 60000000 | tf_op jit(solution)/shard_map/diffuse/pallas_call | solution.py:465
Async XLA Ops:
  111.7 15.1 %collective-permute-start.32 = (f32[56,768]{1,0:T(8,128)}, f32[56,768]{1,0:T(8,128)S(1)}, u32[]{:S(2)}, u32[]{:S(2)}) collective-permute-start(f32[56,768]{1,0:T(8,128)} %get-tuple-element.123), channel_id=1, source_target_pairs={{0,1},{1,2},{2,3},{3,4},{4,5},{5,6},{6,7},{7,8},{8,9},{9,10},{10,1... | collective-permute-start | bytes 516104 | tf_op jit(solution)/shard_map/ppermute | solution.py:513
  111.7 15.0 %collective-permute-start.33 = (f32[56,384]{1,0:T(8,128)}, f32[56,384]{1,0:T(8,128)S(1)}, u32[]{:S(2)}, u32[]{:S(2)}) collective-permute-start(f32[56,384]{1,0:T(8,128)} %get-tuple-element.124), channel_id=1, source_target_pairs={{1,0},{2,1},{3,2},{4,3},{5,4},{6,5},{7,6},{8,7},{9,8},{10,9},{11,1... | collective-permute-start | bytes 258056 | tf_op jit(solution)/shard_map/ppermute | solution.py:514
  117.3 16.7 %all-to-all-start.1 = ((f32[128,1,128]{2,1,0:T(1,128)}), f32[128,1,128]{2,1,0:T(1,128)S(1)}, u32[]{:S(2)}, u32[]{:S(2)}) async-start(f32[128,1,128]{2,1,0:T(1,128)} %get-tuple-element.128), calls=%async_computation.1 | async-start | bytes 131072 | tf_op jit(solution)/shard_map/all_to_all | solution.py:517
  126.7 0.6 copy-start.1
  126.8 0.7 copy-start
  135.4 5.8 %collective-permute-start.18 = (f32[5,56,128]{2,1,0:T(8,128)S(1)}, f32[5,56,128]{2,1,0:T(8,128)}, u32[]{:S(2)}, u32[]{:S(2)}) collective-permute-start(f32[5,56,128]{2,1,0:T(8,128)S(1)} %get-tuple-element.82), channel_id=1, source_target_pairs={{0,16},{1,17},{2,18},{3,19},{4,20},{5,21},{6,22},{7,23},{8,24},{9,... | collective-permute-start | bytes 430088 | tf_op jit(solution)/shard_map/cond/branch_9_fun/ppermute | solution.py:528
  136.4 9.4 %collective-permute-start.19 = (f32[5,56,128]{2,1,0:T(8,128)S(1)}, f32[5,56,128]{2,1,0:T(8,128)}, u32[]{:S(2)}, u32[]{:S(2)}) collective-permute-start(f32[5,56,128]{2,1,0:T(8,128)S(1)} %get-tuple-element.83), channel_id=1, source_target_pairs={{16,32},{17,33},{18,34},{19,35},{20,36},{21,37},{22,38},{23,39},{2... | collective-permute-start | bytes 430088 | tf_op jit(solution)/shard_map/cond/branch_9_fun/ppermute | solution.py:529

commit v2 on v0

--- a/solution.py
+++ b/solution.py
@@ -27,6 +27,7 @@
     out_ref,
     bgm_ref,
     info_ref,
+    turn_ref,
     order_ref,
     counts_ref,
 ):
@@ -56,7 +57,9 @@
                 x = jnp.where(least, jnp.minimum(x, other), jnp.maximum(x, other))
                 step //= 2
             size *= 2
-        order_ref[...] = x.astype(jnp.int32) & (n - 1)
+        order = x.astype(jnp.int32) & (n - 1)
+        here = lax.axis_index("lat") * lax.axis_size("lon") + lax.axis_index("lon")
+        order_ref[...] = jnp.take_along_axis(order, lane ^ (16 * (here % 8)), axis=1)
 
     span = n * lax.axis_size("lon")
     moved = (partner_ref[0] + (span - 3)) % span
@@ -64,7 +67,8 @@
     info_ref[0] = moved % n
     info_ref[1] = 1 - lat_at % 2
     info_ref[2] = (lat_at == lax.axis_size("lat") - 1).astype(jnp.int32)
-    info_ref[3] = moved // n
+    info_ref[3] = 0
+    turn_ref[0] = moved // n
 
     for p in range(2):
         for k in range(0, levels, 2):
@@ -105,6 +109,7 @@
             jax.ShapeDtypeStruct((owners * DEEP, n), F32),
             jax.ShapeDtypeStruct((levels * ny, 2 * nx), BF16),
             jax.ShapeDtypeStruct((4,), jnp.int32),
+            jax.ShapeDtypeStruct((1,), jnp.int32),
         ),
         in_specs=[
             smem(),
@@ -119,6 +124,7 @@
             pl.BlockSpec((some * DEEP, n), lambda i: (i, 0)),
             pl.BlockSpec((levels * ny // steps, 2 * nx), lambda i: (i, 0)),
             smem(),
+            smem(),
         ),
         scratch_shapes=[pltpu.VMEM((owners, n), jnp.int32), pltpu.VMEM((owners, n), jnp.int32)],
         compiler_params=params(),
@@ -141,14 +147,8 @@
         for r in range(0, 56, 8):
             xs = [rec_ref[pl.ds(pl.multiple_of((eight * 8 + i) * 56 + r, 8), 8), :] for i in range(8)]
             for d in (1, 2, 4):
-                keep = (lane // (16 * d)) % 2 == 0
-                new = list(xs)
-                for i in range(8):
-                    if i & d == 0:
-                        lo, hi = xs[i], xs[i + d]
-                        new[i] = jnp.where(keep, lo, pltpu.roll(hi, 16 * d, axis=1))
-                        new[i + d] = jnp.where(keep, pltpu.roll(lo, 128 - 16 * d, axis=1), hi)
-                xs = new
+                keep = (lane & (16 * d)) == 0
+                xs = [jnp.where(keep, xs[i], xs[i ^ d]) for i in range(8)]
             for i in range(8):
                 tiles[i, r : r + 8, pl.ds(pl.multiple_of(eight * 128, 128), 128)] = xs[i]
         return 0
@@ -499,10 +499,10 @@
     owners = obs_weight.shape[1]
     bg = background.reshape(levels, ny, nx)
     es = error_scale.reshape(levels, ny, nx)
-    packed, bgm, info = pack_call(
+    packed, bgm, info, turn = pack_call(
         partner, obs_count, jnp.swapaxes(obs_weight[0], 0, 1), obs_value[0], obs_error[0], obs_column[0], bg
     )
-    turn = info[3]
+    turn = turn.reshape(())
     packed, bgm, info, turn = lax.optimization_barrier((packed, bgm, info, turn))
     received = lax.all_to_all(packed, ("lat", "lon"), split_axis=0, concat_axis=0, tiled=True)
     state, to_east, to_west, cost = observe_call(received, bgm, east_rate, north_rate, sea_mask, es)

time: 166 us -> 161 us (0.970)
  Pallas kernels: 76.1 us -> 69.3 us
  starting transfers between devices: 18.4 us -> 22.3 us
    pallas_call x1, Pallas kernels: 48.1 us -> 41.3 us  [observe_call(): pl.pallas_call(observe, out_shape=(jax.ShapeDtypeStruct((ny * DEEP, nx),...]
    all_to_all x1, starting transfers between devices: 8.01 us -> 11.6 us  [run(): lax.all_to_all(cost, ('lat', 'lon'), split_axis=0, concat_axis=0, tiled=T...]
where the time goes in v2:
time: 161 us; the launch traced here: 159 us
  Pallas kernels  69.3 us (43%)
  blocking collectives  56.3 us (35%)
  starting transfers between devices  22.3 us (14%)
  waiting for transfers between devices  6.87 us (4%)
  between operations  2.42 us (2%)
    all_to_all x1, blocking collectives, shards(): lax.all_to_all(packed, ('lat', 'lon'), split_axis=0, concat_axis=0, tiled...  56.3 us
    pallas_call x1, Pallas kernels, observe_call(): pl.pallas_call(observe, out_shape=(jax.ShapeDtypeStruct((ny * DEEP, nx),...  41.3 us
    pallas_call x1, Pallas kernels, diffuse_call(): pl.pallas_call(diffuse, out_shape=jax.ShapeDtypeStruct((levels * ny, nx),...  17.4 us
    all_to_all x1, starting transfers between devices, run(): lax.all_to_all(cost, ('lat', 'lon'), split_axis=0, concat_axis=0, tiled=T...  11.6 us
    pallas_call x1, Pallas kernels, pack_call(): pl.pallas_call(pack, grid=(steps,), out_shape=(jax.ShapeDtypeStruct((owne...  7.91 us
    ppermute x1, starting transfers between devices, shards(): lax.ppermute(to_west, 'lon', [((i + 1) % n_lon, i) for i in range(n_lon)])  5.03 us
    ppermute x1, starting transfers between devices, run(): got_two = lax.ppermute(two, ('lat', 'lon'), perm_of(n_lat, n_lon, rule))  4.1 us
  transfers between devices with their start and end apart: 5, of which 4 were waited for; matrix products, arithmetic and copies ran while one was open for 0% of the time, Pallas kernels for 0%

profile of v2, /device:TPU:6, one launch (start us, length us, event | category | flops | bytes accessed | tf_op | source)
XLA Modules:
  0.0 159.5 jit_solution(1528696909228766248)
XLA Ops:
  0.6 7.9 %pack.1 = (f32[7168,128]{1,0:T(8,128)}, bf16[3200,256]{1,0:T(8,128)(2,1)}, s32[4]{0:T(128)}, s32[1]{0:T(128)}) custom-call(s32[2048]{0:T(1024)} %partner_ref.1, s32[1,128]{1,0:T(1,128)} %count_ref.1, f32[50,128,128]{2,1,0:T(8,128)} %bitcast.21, f32[128,128]{1,0:T(8,128)} %bitcast.24, f32[128,128]{1,0:T(8,128)} %bitcast.25, s32[128,128]{1,0:T(8,128)} %bitcast.26, ...), custom_call_target="tpu_custom_call" | custom-call | tf_op jit(solution)/shard_map/pack/pallas_call | solution.py:105
  8.5 56.3 %all_to_all.75 = f32[128,56,128]{2,1,0:T(8,128)} all-to-all(f32[128,56,128]{2,1,0:T(8,128)} %bitcast.20), channel_id=1, replica_groups=mesh['lat'=8,'lon'=16] {'lat','lon'}, dimensions={0} | all-to-all | bytes 7340032 | tf_op jit(solution)/shard_map/all_to_all | solution.py:507
  64.8 41.3 %observe.1 = (f32[3584,128]{1,0:T(8,128)}, f32[56,768]{1,0:T(8,128)}, f32[56,384]{1,0:T(8,128)}, f32[128,1,128]{2,1,0:T(1,128)}) custom-call(f32[7168,128]{1,0:T(8,128)} %bitcast.17, bf16[3200,256]{1,0:T(8,128)(2,1)} %get-tuple-element.170.bgm_ref, f32[64,128]{1,0:T(8,128)} %east_ref.1, f32[64,128]{1,0:T(8,128)} %north_ref.1, s32[64,128]{1,0:T(8,128)} %sea_ref.1, ...), custom_call_target="tpu_custom_call" | custom-call | tf_op jit(solution)/shard_map/observe/pallas_call | solution.py:278
  106.1 0.6 collective-permute-start.32
  106.7 5.0 %collective-permute-start.33 = (f32[56,384]{1,0:T(8,128)}, f32[56,384]{1,0:T(8,128)S(1)}, u32[]{:S(2)}, u32[]{:S(2)}) collective-permute-start(f32[56,384]{1,0:T(8,128)} %get-tuple-element.173), channel_id=1, source_target_pairs={{1,0},{2,1},{3,2},{4,3},{5,4},{6,5},{7,6},{8,7},{9,8},{10,9},{11,1... | collective-permute-start | bytes 258056 | tf_op jit(solution)/shard_map/ppermute | solution.py:514
  112.4 1.8 %collective-permute-done.33.fe_ref = f32[56,384]{1,0:T(8,128)S(1)} collective-permute-done((f32[56,384]{1,0:T(8,128)}, f32[56,384]{1,0:T(8,128)S(1)}, u32[]{:S(2)}, u32[]{:S(2)}) %collective-permute-start.33) | collective-permute-done | bytes 86048 | tf_op jit(solution)/shard_map/ppermute | solution.py:514
  114.2 0.0 copy-start.1
  114.2 0.9 collective-permute-done.32.fw_ref
  115.1 0.0 copy-start
  115.1 0.0 copy-done.1
  115.1 0.7 copy-done
  115.8 2.7 %assemble.1 = (f32[5,56,128]{2,1,0:T(8,128)S(1)}, f32[5,56,128]{2,1,0:T(8,128)S(1)}) custom-call(s32[4]{0:T(128)} %get-tuple-element.168.info_ref, f32[64,56,128]{2,1,0:T(8,128)} %bitcast.14, f32[64,56,128]{2,1,0:T(8,128)} %bitcast.15, f32[56,768]{1,0:T(8,128)} %copy-done, f32[56,384]{1,0:T(8,128)} %copy-done.1), custom_call_target="tpu_custom_call" | custom-call | tf_op jit(solution)/shard_map/assemble/pallas_call | solution.py:446
  118.5 22.4 %conditional.1 = (f32[5,56,128]{2,1,0:T(8,128)}, f32[5,56,128]{2,1,0:T(8,128)}, f32[]{:T(128)}) conditional(s32[]{:T(128)} %clamp.3, (f32[5,56,128]{2,1,0:T(8,128)S(1)}, f32[5,56,128]{2,1,0:T(8,128)S(1)}, f32[128,1,128]{2,1,0:T(1,128)}) %tuple.90, (f32[5,56,128]{2,1,0:T(8,128)S(1)}, f32[5,56,128]{2,1,0:T(8,128)S(1)}, ...), branch_computations={%region_0.2_spmd, %region_2.4_spmd, %region_4.6_spmd, %region_6.8_... | conditional | flops 128 | bytes 1344152 | solution.py:533
  118.7 11.6 %all-to-all-start.11 = ((f32[128,1,128]{2,1,0:T(1,128)}), f32[128,1,128]{2,1,0:T(1,128)S(1)}, u32[]{:S(2)}, u32[]{:S(2)}) async-start(f32[128,1,128]{2,1,0:T(1,128)} %get-tuple-element.132), calls=%async_computation.11 | async-start | bytes 131072 | tf_op jit(solution)/shard_map/cond/branch_11_fun/all_to_all | solution.py:528
  130.3 0.9 collective-permute-start.22
  131.2 4.1 %collective-permute-start.23 = (f32[5,56,128]{2,1,0:T(8,128)S(1)}, f32[5,56,128]{2,1,0:T(8,128)}, u32[]{:S(2)}, u32[]{:S(2)}) collective-permute-start(f32[5,56,128]{2,1,0:T(8,128)S(1)} %get-tuple-element.131), channel_id=1, source_target_pairs={{16,32},{17,33},{18,34},{19,35},{20,36},{21,37},{22,38},{23,39},{2... | collective-permute-start | bytes 430088 | tf_op jit(solution)/shard_map/cond/branch_11_fun/ppermute | solution.py:527
  135.3 2.9 %all-to-all-done.11 = f32[128,1,128]{2,1,0:T(1,128)S(1)} async-done(((f32[128,1,128]{2,1,0:T(1,128)}), f32[128,1,128]{2,1,0:T(1,128)S(1)}, u32[]{:S(2)}, u32[]{:S(2)}) %all-to-all-start.11) | async-done | bytes 65568 | tf_op jit(solution)/shard_map/cond/branch_11_fun/all_to_all | solution.py:528
  138.2 0.7 slice_reduce_fusion.11
  139.6 0.0 collective-permute-done.22
  139.6 1.3 collective-permute-done.23
  140.9 17.4 %diffuse.1 = f32[3200,128]{1,0:T(8,128)} custom-call(s32[4]{0:T(128)} %get-tuple-element.168.info_ref, f32[64,56,128]{2,1,0:T(8,128)} %bitcast.16, f32[56,768]{1,0:T(8,128)} %copy-done, f32[56,384]{1,0:T(8,128)} %copy-done.1, f32[5,56,128]{2,1,0:T(8,128)} %get-tuple-element.178.one_ref, f32[5,56,128]{2,1,0:T(8,128)} %get-tuple-element.179.two_ref, ...), custom_call_target="tpu_custom_call" | custom-call | flops 32768000 | bytes 60000000 | tf_op jit(solution)/shard_map/diffuse/pallas_call | solution.py:465
Async XLA Ops:
  106.1 9.0 %collective-permute-start.32 = (f32[56,768]{1,0:T(8,128)}, f32[56,768]{1,0:T(8,128)S(1)}, u32[]{:S(2)}, u32[]{:S(2)}) collective-permute-start(f32[56,768]{1,0:T(8,128)} %get-tuple-element.172), channel_id=1, source_target_pairs={{0,1},{1,2},{2,3},{3,4},{4,5},{5,6},{6,7},{7,8},{8,9},{9,10},{10,1... | collective-permute-start | bytes 516104 | tf_op jit(solution)/shard_map/ppermute | solution.py:513
  106.7 7.4 %collective-permute-start.33 = (f32[56,384]{1,0:T(8,128)}, f32[56,384]{1,0:T(8,128)S(1)}, u32[]{:S(2)}, u32[]{:S(2)}) collective-permute-start(f32[56,384]{1,0:T(8,128)} %get-tuple-element.173), channel_id=1, source_target_pairs={{1,0},{2,1},{3,2},{4,3},{5,4},{6,5},{7,6},{8,7},{9,8},{10,9},{11,1... | collective-permute-start | bytes 258056 | tf_op jit(solution)/shard_map/ppermute | solution.py:514
  114.2 0.9 copy-start.1
  115.1 0.7 copy-start
  118.7 19.6 %all-to-all-start.11 = ((f32[128,1,128]{2,1,0:T(1,128)}), f32[128,1,128]{2,1,0:T(1,128)S(1)}, u32[]{:S(2)}, u32[]{:S(2)}) async-start(f32[128,1,128]{2,1,0:T(1,128)} %get-tuple-element.132), calls=%async_computation.11 | async-start | bytes 131072 | tf_op jit(solution)/shard_map/cond/branch_11_fun/all_to_all | solution.py:528
  130.3 9.3 %collective-permute-start.22 = (f32[5,56,128]{2,1,0:T(8,128)S(1)}, f32[5,56,128]{2,1,0:T(8,128)}, u32[]{:S(2)}, u32[]{:S(2)}) collective-permute-start(f32[5,56,128]{2,1,0:T(8,128)S(1)} %get-tuple-element.130), channel_id=1, source_target_pairs={{0,16},{1,17},{2,18},{3,19},{4,20},{5,21},{6,22},{7,23},{8,24},{9,... | collective-permute-start | bytes 430088 | tf_op jit(solution)/shard_map/cond/branch_11_fun/ppermute | solution.py:526
  131.2 9.7 %collective-permute-start.23 = (f32[5,56,128]{2,1,0:T(8,128)S(1)}, f32[5,56,128]{2,1,0:T(8,128)}, u32[]{:S(2)}, u32[]{:S(2)}) collective-permute-start(f32[5,56,128]{2,1,0:T(8,128)S(1)} %get-tuple-element.131), channel_id=1, source_target_pairs={{16,32},{17,33},{18,34},{19,35},{20,36},{21,37},{22,38},{23,39},{2... | collective-permute-start | bytes 430088 | tf_op jit(solution)/shard_map/cond/branch_11_fun/ppermute | solution.py:527

commit v3 on v2

--- a/solution.py
+++ b/solution.py
@@ -514,6 +514,8 @@
     from_east = lax.ppermute(to_west, "lon", [((i + 1) % n_lon, i) for i in range(n_lon)])
     one, two = assemble_call(info, state, from_west, from_east)
 
+    shares = lax.all_to_all(cost, ("lat", "lon"), split_axis=0, concat_axis=0, tiled=True)
+
     def branch(q):
         def rule(a, b):
             if a == n_lat - 1:
@@ -522,17 +524,18 @@
                 return None
             return (((a + 1) ^ 1) - 1, b)
 
-        def run(one, two, cost):
+        def run(one, two):
             got_one = lax.ppermute(one, ("lat", "lon"), perm_of(n_lat, n_lon, lambda a, b: (a ^ 1, b)))
             got_two = lax.ppermute(two, ("lat", "lon"), perm_of(n_lat, n_lon, rule))
-            shares = lax.all_to_all(cost, ("lat", "lon"), split_axis=0, concat_axis=0, tiled=True)
-            return got_one, got_two, shares
+            return got_one, got_two
 
         return run
 
-    got_one, got_two, shares = lax.switch(turn, [branch(q) for q in range(n_lon)], one, two, cost)
+    one, two, shares = lax.optimization_barrier((one, two, shares))
+    got_one, got_two = lax.switch(turn, [branch(q) for q in range(n_lon)], one, two)
+    increment = diffuse_call(info, state, from_west, from_east, got_one, got_two, es)
+    increment, shares = lax.optimization_barrier((increment, shares))
     cost_share = jnp.sum(shares[:, 0, 0]) / (owners * owners * capacity)
-    increment = diffuse_call(info, state, from_west, from_east, got_one, got_two, es)
     return (increment.reshape(background.shape), cost_share)
 
 

time: 161 us -> 160 us (level)
  starting transfers between devices: 22.3 us -> 17.4 us
  waiting for transfers between devices: 6.87 us -> 9.44 us
  Pallas kernels: 69.3 us -> 71 us
    all_to_all x1, starting transfers between devices: 11.6 us -> 7.2 us  [shards(): lax.all_to_all(cost, ('lat', 'lon'), split_axis=0, concat_axis=0, tiled=T...]
    ppermute x1, waiting for transfers between devices: 1.28 us -> 4.59 us  [run(): got_two = lax.ppermute(two, ('lat', 'lon'), perm_of(n_lat, n_lon, rule))]
    ppermute x1, waiting for transfers between devices: 1.76 us -> 0.01 us  [shards(): lax.ppermute(to_west, 'lon', [((i + 1) % n_lon, i) for i in range(n_lon)])]
    pallas_call x1, Pallas kernels: 41.3 us -> 43 us  [observe_call(): pl.pallas_call(observe, out_shape=(jax.ShapeDtypeStruct((ny * DEEP, nx),...]
  transfers between devices with their start and end apart: 5 -> 5, of which waited for: 4 -> 3; matrix products, arithmetic and copies ran while one was open for 0% -> 0% of each run, Pallas kernels for 0% -> 2%
where the time goes in v3:
time: 160 us; the launch traced here: 159 us
  Pallas kernels  71 us (44%)
  blocking collectives  56.3 us (35%)
  starting transfers between devices  17.4 us (11%)
  waiting for transfers between devices  9.44 us (6%)
  between operations  3 us (2%)
    all_to_all x1, blocking collectives, shards(): lax.all_to_all(packed, ('lat', 'lon'), split_axis=0, concat_axis=0, tiled...  56.3 us
    pallas_call x1, Pallas kernels, observe_call(): pl.pallas_call(observe, out_shape=(jax.ShapeDtypeStruct((ny * DEEP, nx),...  43 us
    pallas_call x1, Pallas kernels, diffuse_call(): pl.pallas_call(diffuse, out_shape=jax.ShapeDtypeStruct((levels * ny, nx),...  17.4 us
    pallas_call x1, Pallas kernels, pack_call(): pl.pallas_call(pack, grid=(steps,), out_shape=(jax.ShapeDtypeStruct((owne...  7.91 us
    all_to_all x1, starting transfers between devices, shards(): lax.all_to_all(cost, ('lat', 'lon'), split_axis=0, concat_axis=0, tiled=T...  7.2 us
    ppermute x1, starting transfers between devices, shards(): lax.ppermute(to_west, 'lon', [((i + 1) % n_lon, i) for i in range(n_lon)])  5.36 us
    ppermute x1, waiting for transfers between devices, run(): got_two = lax.ppermute(two, ('lat', 'lon'), perm_of(n_lat, n_lon, rule))  4.59 us
    all_to_all x1, waiting for transfers between devices, shards(): lax.all_to_all(cost, ('lat', 'lon'), split_axis=0, concat_axis=0, tiled=T...  4.03 us
  transfers between devices with their start and end apart: 5, of which 3 were waited for; matrix products, arithmetic and copies ran while one was open for 0% of the time, Pallas kernels for 2%

profile of v3, /device:TPU:6, one launch (start us, length us, event | category | flops | bytes accessed | tf_op | source)
XLA Modules:
  0.0 158.6 jit_solution(5599501546592739487)
XLA Ops:
  0.6 7.9 %pack.1 = (f32[7168,128]{1,0:T(8,128)}, bf16[3200,256]{1,0:T(8,128)(2,1)}, s32[4]{0:T(128)}, s32[1]{0:T(128)}) custom-call(s32[2048]{0:T(1024)} %partner_ref.1, s32[1,128]{1,0:T(1,128)} %count_ref.1, f32[50,128,128]{2,1,0:T(8,128)} %bitcast.22, f32[128,128]{1,0:T(8,128)} %bitcast.25, f32[128,128]{1,0:T(8,128)} %bitcast.26, s32[128,128]{1,0:T(8,128)} %bitcast.27, ...), custom_call_target="tpu_custom_call" | custom-call | tf_op jit(solution)/shard_map/pack/pallas_call | solution.py:105
  8.5 56.3 %all_to_all.16 = f32[128,56,128]{2,1,0:T(8,128)} all-to-all(f32[128,56,128]{2,1,0:T(8,128)} %bitcast.21), channel_id=1, replica_groups=mesh['lat'=8,'lon'=16] {'lat','lon'}, dimensions={0} | all-to-all | bytes 7340032 | tf_op jit(solution)/shard_map/all_to_all | solution.py:507
  64.8 43.0 %observe.1 = (f32[3584,128]{1,0:T(8,128)}, f32[56,768]{1,0:T(8,128)}, f32[56,384]{1,0:T(8,128)}, f32[128,1,128]{2,1,0:T(1,128)}) custom-call(f32[7168,128]{1,0:T(8,128)} %bitcast.18, bf16[3200,256]{1,0:T(8,128)(2,1)} %get-tuple-element.125.bgm_ref, f32[64,128]{1,0:T(8,128)} %east_ref.1, f32[64,128]{1,0:T(8,128)} %north_ref.1, s32[64,128]{1,0:T(8,128)} %sea_ref.1, ...), custom_call_target="tpu_custom_call" | custom-call | tf_op jit(solution)/shard_map/observe/pallas_call | solution.py:278
  107.8 0.0 collective-permute-start.32
  107.8 5.4 %collective-permute-start.33 = (f32[56,384]{1,0:T(8,128)}, f32[56,384]{1,0:T(8,128)S(1)}, u32[]{:S(2)}, u32[]{:S(2)}) collective-permute-start(f32[56,384]{1,0:T(8,128)} %get-tuple-element.128), channel_id=1, source_target_pairs={{1,0},{2,1},{3,2},{4,3},{5,4},{6,5},{7,6},{8,7},{9,8},{10,9},{11,1... | collective-permute-start | bytes 258056 | tf_op jit(solution)/shard_map/ppermute | solution.py:514
  113.2 7.2 %all-to-all-start.1 = ((f32[128,1,128]{2,1,0:T(1,128)}), f32[128,1,128]{2,1,0:T(1,128)S(1)}, u32[]{:S(2)}, u32[]{:S(2)}) async-start(f32[128,1,128]{2,1,0:T(1,128)} %get-tuple-element.132), calls=%async_computation.1 | async-start | bytes 131072 | tf_op jit(solution)/shard_map/all_to_all | solution.py:517
  120.9 0.0 collective-permute-done.33.fe_ref
  121.0 0.0 copy-start.1
  121.0 0.0 collective-permute-done.32.fw_ref
  121.0 0.0 copy-start
  121.0 0.6 copy-done.1
  121.6 0.1 copy-done
  121.6 2.7 %assemble.1 = (f32[5,56,128]{2,1,0:T(8,128)S(1)}, f32[5,56,128]{2,1,0:T(8,128)S(1)}) custom-call(s32[4]{0:T(128)} %get-tuple-element.123.info_ref, f32[64,56,128]{2,1,0:T(8,128)} %bitcast.15, f32[64,56,128]{2,1,0:T(8,128)} %bitcast.16, f32[56,768]{1,0:T(8,128)} %copy-done, f32[56,384]{1,0:T(8,128)} %copy-done.1), custom_call_target="tpu_custom_call" | custom-call | tf_op jit(solution)/shard_map/assemble/pallas_call | solution.py:446
  124.3 4.0 %all-to-all-done.1 = f32[128,1,128]{2,1,0:T(1,128)S(1)} async-done(((f32[128,1,128]{2,1,0:T(1,128)}), f32[128,1,128]{2,1,0:T(1,128)S(1)}, u32[]{:S(2)}, u32[]{:S(2)}) %all-to-all-start.1) | async-done | bytes 65568 | tf_op jit(solution)/shard_map/all_to_all | solution.py:517
  128.3 10.3 %conditional.1 = (f32[5,56,128]{2,1,0:T(8,128)}, f32[5,56,128]{2,1,0:T(8,128)}) conditional(s32[]{:T(128)} %clamp.3, (f32[5,56,128]{2,1,0:T(8,128)S(1)}, f32[5,56,128]{2,1,0:T(8,128)S(1)}) %assemble.1, (f32[5,56,128]{2,1,0:T(8,128)S(1)}, f32[5,56,128]{2,1,0:T(8,128)S(1)}) %assemble.1, (f32[5,56,128]{2,1,0:T(8,128)S(1)}, ...), branch_computations={%region_0.0_spmd, %region_1.0_spmd, %region_2.0_spmd, %region_3.0_... | conditional | bytes 1146976 | solution.py:535
  128.3 0.9 collective-permute-start.26
  129.2 4.0 %collective-permute-start.27 = (f32[5,56,128]{2,1,0:T(8,128)S(1)}, f32[5,56,128]{2,1,0:T(8,128)}, u32[]{:S(2)}, u32[]{:S(2)}) collective-permute-start(f32[5,56,128]{2,1,0:T(8,128)S(1)} %get-tuple-element.91), channel_id=1, source_target_pairs={{16,32},{17,33},{18,34},{19,35},{20,36},{21,37},{22,38},{23,39},{2... | collective-permute-start | bytes 430088 | tf_op jit(solution)/shard_map/cond/branch_13_fun/ppermute | solution.py:529
  133.2 0.8 collective-permute-done.26
  134.0 4.6 %collective-permute-done.27 = f32[5,56,128]{2,1,0:T(8,128)} collective-permute-done((f32[5,56,128]{2,1,0:T(8,128)S(1)}, f32[5,56,128]{2,1,0:T(8,128)}, u32[]{:S(2)}, u32[]{:S(2)}) %collective-permute-start.27) | collective-permute-done | bytes 143392 | tf_op jit(solution)/shard_map/cond/branch_13_fun/ppermute | solution.py:529
  138.6 17.4 %diffuse.1 = f32[3200,128]{1,0:T(8,128)} custom-call(s32[4]{0:T(128)} %get-tuple-element.123.info_ref, f32[64,56,128]{2,1,0:T(8,128)} %bitcast.17, f32[56,768]{1,0:T(8,128)} %copy-done, f32[56,384]{1,0:T(8,128)} %copy-done.1, f32[5,56,128]{2,1,0:T(8,128)} %get-tuple-element.135.one_ref, f32[5,56,128]{2,1,0:T(8,128)} %get-tuple-element.136.two_ref, ...), custom_call_target="tpu_custom_call" | custom-call | flops 32768000 | bytes 60000000 | tf_op jit(solution)/shard_map/diffuse/pallas_call | solution.py:465
  156.1 0.7 slice_reduce_fusion
Async XLA Ops:
  107.8 13.1 %collective-permute-start.32 = (f32[56,768]{1,0:T(8,128)}, f32[56,768]{1,0:T(8,128)S(1)}, u32[]{:S(2)}, u32[]{:S(2)}) collective-permute-start(f32[56,768]{1,0:T(8,128)} %get-tuple-element.127), channel_id=1, source_target_pairs={{0,1},{1,2},{2,3},{3,4},{4,5},{5,6},{6,7},{7,8},{8,9},{9,10},{10,1... | collective-permute-start | bytes 516104 | tf_op jit(solution)/shard_map/ppermute | solution.py:513
  107.8 13.1 %collective-permute-start.33 = (f32[56,384]{1,0:T(8,128)}, f32[56,384]{1,0:T(8,128)S(1)}, u32[]{:S(2)}, u32[]{:S(2)}) collective-permute-start(f32[56,384]{1,0:T(8,128)} %get-tuple-element.128), channel_id=1, source_target_pairs={{1,0},{2,1},{3,2},{4,3},{5,4},{6,5},{7,6},{8,7},{9,8},{10,9},{11,1... | collective-permute-start | bytes 258056 | tf_op jit(solution)/shard_map/ppermute | solution.py:514
  113.2 15.2 %all-to-all-start.1 = ((f32[128,1,128]{2,1,0:T(1,128)}), f32[128,1,128]{2,1,0:T(1,128)S(1)}, u32[]{:S(2)}, u32[]{:S(2)}) async-start(f32[128,1,128]{2,1,0:T(1,128)} %get-tuple-element.132), calls=%async_computation.1 | async-start | bytes 131072 | tf_op jit(solution)/shard_map/all_to_all | solution.py:517
  121.0 0.6 copy-start.1
  121.0 0.7 copy-start
  128.3 5.7 %collective-permute-start.26 = (f32[5,56,128]{2,1,0:T(8,128)S(1)}, f32[5,56,128]{2,1,0:T(8,128)}, u32[]{:S(2)}, u32[]{:S(2)}) collective-permute-start(f32[5,56,128]{2,1,0:T(8,128)S(1)} %get-tuple-element.90), channel_id=1, source_target_pairs={{0,16},{1,17},{2,18},{3,19},{4,20},{5,21},{6,22},{7,23},{8,24},{9,... | collective-permute-start | bytes 430088 | tf_op jit(solution)/shard_map/cond/branch_13_fun/ppermute | solution.py:528
  129.2 9.4 %collective-permute-start.27 = (f32[5,56,128]{2,1,0:T(8,128)S(1)}, f32[5,56,128]{2,1,0:T(8,128)}, u32[]{:S(2)}, u32[]{:S(2)}) collective-permute-start(f32[5,56,128]{2,1,0:T(8,128)S(1)} %get-tuple-element.91), channel_id=1, source_target_pairs={{16,32},{17,33},{18,34},{19,35},{20,36},{21,37},{22,38},{23,39},{2... | collective-permute-start | bytes 430088 | tf_op jit(solution)/shard_map/cond/branch_13_fun/ppermute | solution.py:529
